TPU v7x, 32 devices: a whole 2x2x4 slice. The times are simulated.
32 devices in a mesh: fsdp: 16 (over z, y, core), ctx: 2 (over x).
Axes of the slice: x: 2, y: 2, z: 4, core: 2. Of those that a mesh axis runs over, the one named last changes fastest.
Arguments:
- queries: bfloat16 [3328, 3072], P(('fsdp', 'ctx')), may hold values from -6 to 6
- keys: bfloat16 [3328, 3072], P(('fsdp', 'ctx')), may hold values from -6 to 6
- values: bfloat16 [3328, 3072], P(('fsdp', 'ctx')), may hold values from -6 to 6
- norm_gain: float32 [3072], replicated, may hold values from 0.1 to 1.9
- out_weight: bfloat16 [3072, 3072], P('fsdp', 'ctx'), may hold values from -0.109375 to 0.109375
Outputs:
- layer_out: bfloat16 [3328, 3072], P('fsdp', 'ctx')
All inputs are finite; a program needn't handle non-finite values.
Results may differ from a plain program's by a relative error of at most 0.0061.
Values may be sent and summed in bfloat16 or wider, within the bound.
A program may use at most 64 MiB of HBM per device.

v0:
```python
import jax
import jax.numpy as jnp
from jax import lax
from jax.sharding import PartitionSpec as P

HEADS = 32
HEAD_DIM = 96


def on_device(queries, keys, values, norm_gain, out_weight):
    tok_rows = queries.shape[0]
    q_heads = queries.reshape(tok_rows, HEADS, HEAD_DIM)
    k_heads = keys.reshape(tok_rows, HEADS, HEAD_DIM)
    v_heads = values.reshape(tok_rows, HEADS, HEAD_DIM)
    scores = jnp.einsum("thd,shd->hts", q_heads, k_heads, preferred_element_type=jnp.float32)
    causal = jnp.arange(tok_rows)[:, None] >= jnp.arange(tok_rows)[None, :]
    scores = jnp.where(causal, scores, 0.0).astype(jnp.bfloat16)
    intra = jnp.einsum("hts,shd->thd", scores, v_heads, preferred_element_type=jnp.float32)
    local_state = jnp.einsum("shd,she->hde", k_heads, v_heads, preferred_element_type=jnp.float32)
    flat_state = local_state.reshape(HEADS, HEAD_DIM * HEAD_DIM).astype(jnp.bfloat16)
    every_state = lax.all_gather(flat_state[None], "ctx", axis=0, tiled=True)
    position = lax.axis_index("ctx")
    earlier = (jnp.arange(every_state.shape[0]) < position)[:, None, None]
    prefix_flat = jnp.sum(jnp.where(earlier, every_state.astype(jnp.float32), 0.0), axis=0)
    prefix_state = prefix_flat.reshape(HEADS, HEAD_DIM, HEAD_DIM).astype(jnp.bfloat16)
    inter = jnp.einsum("thd,hde->the", q_heads, prefix_state, preferred_element_type=jnp.float32)
    attn = (intra + inter).reshape(tok_rows, HEADS * HEAD_DIM)
    mean_sq = jnp.mean(attn * attn, axis=-1, keepdims=True)
    normed = (attn * lax.rsqrt(mean_sq + 1e-05) * norm_gain).astype(jnp.bfloat16)
    weight_block = lax.all_gather(out_weight, "fsdp", axis=0, tiled=True)
    result = jnp.dot(
        lax.all_gather(normed, "ctx", axis=0, tiled=True),
        weight_block,
        preferred_element_type=jnp.float32,
    )
    return result.astype(jnp.bfloat16)


def solution(mesh):
    placed = (
        P(("fsdp", "ctx"), None),
        P(("fsdp", "ctx"), None),
        P(("fsdp", "ctx"), None),
        P(),
        P("fsdp", "ctx"),
    )
    return jax.shard_map(
        on_device, mesh=mesh, in_specs=placed, out_specs=P("fsdp", "ctx"), check_vma=False
    )
```

profile of v0, /device:TPU:0, one launch (start us, length us, event | category | flops | bytes accessed | tf_op | source)
XLA Modules:
  0.0 167.3 jit_solution(5352595424225260672)
XLA Ops:
  6.5 0.0 all-gather.4.cloned.1.call-start
  6.5 1.5 copy.25
  8.1 0.0 copy-done.1
  8.1 0.4 copy.26
  8.5 0.7 convolution_convert_fusion.1
  9.1 0.0 copy-start.2
  9.1 1.9 %convert_element_type.33 = bf16[1,32,9216]{2,1,0:T(8,128)(2,1)} reshape(bf16[32,96,96]{2,1,0:T(8,128)(2,1)S(1)} %convolution_convert_fusion.1) | data formatting | bytes 1179648 | tf_op jit(solution)/shard_map/convert_element_type | solution.py:20
  11.0 0.0 all-gather.4.cloned.1.call-update
  11.0 0.0 all-gather.6.cloned.1.call-start
  11.1 0.0 copy-done.2
  11.1 0.4 copy.24
  11.5 2.3 %fusion = f32[32,104,96]{1,2,0:T(8,128)} fusion(bf16[104,32,96]{0,2,1:T(8,128)(2,1)S(1)} %bitcast.22, bf16[104,32,96]{0,2,1:T(8,128)(2,1)S(1)} %bitcast.17, bf16[104,32,96]{0,2,1:T(8,128)(2,1)S(1)} %bitcast.20, pred[104,104]{1,0:T(8,128)(4,1)S(1)} %iota_compare_fusion), kind=kOutput, calls=%fused_computation.6 | convolution fusion | flops 133599232 | bytes 3205696 | tf_op jit(solution)/shard_map/hts,shd->thd/dot_general | solution.py:18
  13.8 22.8 %all-gather.4.cloned.1.call-done = bf16[2,32,9216]{2,1,0:T(8,128)(2,1)} async-done(((bf16[1,32,9216]{2,1,0:T(8,128)(2,1)}), bf16[2,32,9216]{2,1,0:T(8,128)(2,1)}) %all-gather.4.cloned.1.call-update) | async-done | bytes 1179664 | tf_op jit(solution)/shard_map/all_gather | solution.py:21
  36.7 2.6 %select_reduce_fusion = bf16[32,9216]{1,0:T(8,128)(2,1)} fusion(bf16[2,32,9216]{2,1,0:T(8,128)(2,1)} %all-gather.4.cloned.1.call-done, pred[2]{0:T(512)(128)(4,1)S(1)} %iota_compare_fusion.1), kind=kLoop, calls=%fused_computation.1 | loop fusion | flops 1474560 | bytes 1769474 | tf_op jit(solution)/shard_map/reduce_sum | solution.py:24
  39.3 1.8 %convert_element_type.36 = bf16[32,96,96]{2,1,0:T(8,128)(2,1)S(1)} reshape(bf16[32,9216]{1,0:T(8,128)(2,1)} %select_reduce_fusion) | data formatting | bytes 1179648 | tf_op jit(solution)/shard_map/convert_element_type | solution.py:25
  41.1 1.7 %multiply_reduce_fusion = (f32[104]{0:T(128)S(1)}, f32[104,32,96]{0,2,1:T(8,128)}) fusion(bf16[32,96,96]{2,1,0:T(8,128)(2,1)S(1)} %convert_element_type.36, bf16[104,32,96]{0,2,1:T(8,128)(2,1)S(1)} %bitcast.18, f32[32,104,96]{1,2,0:T(8,128)S(1)} %copy-done), kind=kOutput, calls=%fused_computation.4 | convolution fusion | flops 62300056 | bytes 3785120 | tf_op jit(solution)/shard_map/thd,hde->the/dot_general | solution.py:26
  42.9 1.9 %copy.22 = f32[104,3072]{1,0:T(8,128)S(1)} copy(f32[104,3072]{0,1:T(8,128)} %bitcast.23) | data formatting | bytes 2555904 | tf_op jit(solution)/shard_map/reshape | solution.py:27
  44.8 1.0 multiply_convert_fusion
  45.8 0.0 all-gather.6.cloned.1.call-update
  45.8 0.0 all-gather.8.cloned.1.call-start
  45.9 0.7 all-gather.8.cloned.1.call-update
  46.6 23.3 %all-gather.6.cloned.1.call-done = bf16[208,3072]{1,0:T(8,128)(2,1)} async-done(((bf16[104,3072]{1,0:T(8,128)(2,1)}), bf16[208,3072]{1,0:T(8,128)(2,1)}) %all-gather.6.cloned.1.call-update) | async-done | bytes 1277968 | tf_op jit(solution)/shard_map/all_gather | solution.py:32
  69.9 83.8 %all-gather.8.cloned.1.call-done = bf16[3072,1536]{1,0:T(8,128)(2,1)} async-done(((bf16[192,1536]{1,0:T(8,128)(2,1)}), bf16[3072,1536]{1,0:T(8,128)(2,1)}) %all-gather.8.cloned.1.call-update) | async-done | bytes 9437200 | tf_op jit(solution)/shard_map/all_gather | solution.py:30
  153.7 7.1 %convolution_convert_fusion = bf16[208,1536]{1,0:T(8,128)(2,1)} fusion(bf16[208,3072]{1,0:T(8,128)(2,1)} %all-gather.6.cloned.1.call-done, bf16[3072,1536]{1,0:T(8,128)(2,1)} %all-gather.8.cloned.1.call-done), kind=kOutput, calls=%fused_computation | convolution fusion | flops 1963253760 | bytes 11354112 | tf_op jit(solution)/shard_map/dot_general | solution.py:31
  (8 shorter events, 0.0 us)
Async XLA Ops:
  6.5 1.5 copy-start.1
  6.5 30.1 %all-gather.4.cloned.1.call-start = ((), (), s32[]{:S(2)}) async-start(), calls=%async_computation | async-start | bytes 1769472 | tf_op jit(solution)/shard_map/all_gather | solution.py:21
  9.1 2.0 %copy-start.2 = (bf16[104,3072]{1,0:T(8,128)(2,1)S(1)}, bf16[104,3072]{1,0:T(8,128)(2,1)}, u32[]{:S(2)}) copy-start(bf16[104,3072]{1,0:T(8,128)(2,1)} %param.5) | copy-start | bytes 1916932
  11.0 58.8 %all-gather.6.cloned.1.call-start = ((), (), s32[]{:S(2)}) async-start(), calls=%async_computation.1 | async-start | bytes 1916928 | tf_op jit(solution)/shard_map/all_gather | solution.py:32
  13.8 27.3 %copy-start = (f32[32,104,96]{1,2,0:T(8,128)S(1)}, f32[32,104,96]{1,2,0:T(8,128)}, u32[]{:S(2)}) copy-start(f32[32,104,96]{1,2,0:T(8,128)} %fusion) | copy-start | bytes 3833860
  42.9 1.9 %copy-start.3 = (f32[3072]{0:T(1024)S(1)}, f32[3072]{0:T(1024)}, u32[]{:S(2)}) copy-start(f32[3072]{0:T(1024)} %param.8) | copy-start | bytes 36868
  45.8 107.8 %all-gather.8.cloned.1.call-start = ((), (), s32[]{:S(2)}) async-start(), calls=%async_computation.2 | async-start | bytes 10027008 | tf_op jit(solution)/shard_map/all_gather | solution.py:30
Sparse Core Ops, SparseCore 0:
  11.2 25.4 all-gather.3
  46.0 23.8 all-gather.5
  72.2 81.4 all-gather.7
where the time goes:
time: 168 us; the launch traced here: 167 us
  waiting for transfers between devices  131 us (78%)
  between operations  13.2 us (8%)
  matrix products  11.8 us (7%)
  local copies, waits for them, and re-layouts  7.85 us (5%)
  other arithmetic  3.69 us (2%)
    all_gather x1, waiting for transfers between devices, on_device(): weight_block = lax.all_gather(out_weight, 'fsdp', axis=0, tiled=True)  83.8 us
    all_gather x1, waiting for transfers between devices, on_device(): lax.all_gather(normed, 'ctx', axis=0, tiled=True)  23.3 us
    all_gather x1, waiting for transfers between devices, on_device(): every_state = lax.all_gather(flat_state[None], 'ctx', axis=0, tiled=True)  22.8 us
    dot_general x1, matrix products, on_device(): jnp.dot(lax.all_gather(normed, 'ctx', axis=0, tiled=True), weight_block,...  7.07 us
  transfers between devices with their start and end apart: 3, of which 3 were waited for; matrix products, arithmetic and copies ran while one was open for 2% of the time, Pallas kernels for 0%

commit v1 on v0

--- a/solution.py
+++ b/solution.py
@@ -1,10 +1,17 @@
+import functools
+
 import jax
 import jax.numpy as jnp
 from jax import lax
+from jax.experimental import pallas as pl
+from jax.experimental.pallas import tpu as pltpu
 from jax.sharding import PartitionSpec as P
 
 HEADS = 32
 HEAD_DIM = 96
+MESH = pl.DeviceIdType.MESH
+BF16 = jnp.bfloat16
+F32 = jnp.float32
 
 
 def on_device(queries, keys, values, norm_gain, out_weight):
@@ -36,6 +43,334 @@
     return result.astype(jnp.bfloat16)
 
 
+def kernel(
+    planes, q_ref, k_ref, v_ref, gain_ref, w_ref, out_ref,
+    w_all, state_own, state_in, x_out, x_all, x_cat, att, ms, acc, part_out, part_in,
+    w_load, w_send, w_recv, state_send, state_recv, x_send, x_recv, ms_send, ms_recv,
+    part_send, part_recv,
+):
+    tok, features = q_ref.shape
+    rows = w_ref.shape[0]
+    width = 2 * rows
+    chunk = w_ref.shape[1] // planes
+    group_heads = width // HEAD_DIM
+
+    f = lax.axis_index("fsdp")
+    x = lax.axis_index("ctx")
+    z, y, c = lax.div(f, 4), lax.rem(lax.div(f, 2), 2), lax.rem(f, 2)
+
+    def at(zz, yy, cc, xx):
+        return (4 * zz + 2 * yy + cc, xx)
+
+    sibling = at(z, y, 1 - c, x)
+    across = at(z, y, c, 1 - x)
+    beside = at(z, 1 - y, c, x)
+    diagonal = at(z, 1 - y, c, 1 - x)
+
+    def remote(src, dst, send, recv, device):
+        return pltpu.make_async_remote_copy(
+            src_ref=src, dst_ref=dst, send_sem=send, recv_sem=recv,
+            device_id=device, device_id_type=MESH,
+        )
+
+    def load(j):
+        return pltpu.make_async_copy(
+            w_ref.at[:, pl.ds(pl.multiple_of(j * chunk, chunk), chunk)],
+            w_all.at[j, z, c], w_load.at[j],
+        )
+
+    def w_copy(j, plane, way):
+        device = (at(z - 1, y, c, x), at(z + 1, y, c, x), sibling)[way]
+        block = w_all.at[j, plane, c]
+        return remote(block, block, w_send.at[j, plane, way], w_recv.at[j, plane, c], device)
+
+    def w_arrive(j, plane, core):
+        block = w_all.at[j, plane, core]
+        remote(block, block, w_send.at[j, plane, 2], w_recv.at[j, plane, core], sibling).wait_recv()
+
+    def each(body):
+        def step(i, carry):
+            body(i)
+            return carry
+        lax.fori_loop(0, planes, step, 0)
+
+    each(lambda j: load(j).start())
+
+    barrier = pltpu.get_barrier_semaphore()
+    for device in (sibling, across, beside, diagonal):
+        pl.semaphore_signal(barrier, inc=1, device_id=device, device_id_type=MESH)
+
+    @pl.when(z > 0)
+    def _():
+        pl.semaphore_signal(barrier, inc=1, device_id=at(z - 1, y, c, x), device_id_type=MESH)
+
+    @pl.when(z < planes - 1)
+    def _():
+        pl.semaphore_signal(barrier, inc=1, device_id=at(z + 1, y, c, x), device_id_type=MESH)
+
+    pl.semaphore_wait(barrier, 4 + jnp.where(z > 0, 1, 0) + jnp.where(z < planes - 1, 1, 0))
+
+    def send_own(j):
+        load(j).wait()
+
+        @pl.when(z > 0)
+        def _():
+            w_copy(j, z, 0).start()
+
+        @pl.when(z < planes - 1)
+        def _():
+            w_copy(j, z, 1).start()
+
+        w_copy(j, z, 2).start()
+
+    each(send_own)
+
+    lane = lax.broadcasted_iota(jnp.int32, (1, width), 1)
+    in_head = [
+        jnp.where((lane >= h * HEAD_DIM) & (lane < (h + 1) * HEAD_DIM), 1.0, 0.0)
+        for h in range(group_heads)
+    ]
+    in_head16 = [m.astype(BF16) for m in in_head]
+
+    def columns(i, yy):
+        return pl.ds(pl.multiple_of(i * (2 * width), 2 * width) + yy * width, width)
+
+    def state_copy(i, yy):
+        return remote(
+            state_own.at[i, yy], state_in.at[i, yy], state_send.at[i, yy], state_recv.at[i, yy], across
+        )
+
+    @pl.when(x == 0)
+    def _():
+        def states(i):
+            for yy in range(2):
+                full = lax.dot_general(
+                    k_ref[:, columns(i, yy)], v_ref[:, columns(i, yy)],
+                    (((0,), (0,)), ((), ())), preferred_element_type=F32,
+                )
+                folded = full[:HEAD_DIM] * in_head[0]
+                for h in range(1, group_heads):
+                    folded = folded + full[h * HEAD_DIM:(h + 1) * HEAD_DIM] * in_head[h]
+                state_own[i, yy] = folded.astype(BF16)
+                state_copy(i, yy).start()
+        each(states)
+
+    def pass_on(j, distance):
+        @pl.when(z - distance >= 0)
+        def _():
+            w_arrive(j, z - distance, c)
+
+            @pl.when(z < planes - 1)
+            def _():
+                w_copy(j, z - distance, 1).start()
+
+            w_copy(j, z - distance, 2).start()
+
+        @pl.when(z + distance < planes)
+        def _():
+            w_arrive(j, z + distance, c)
+
+            @pl.when(z > 0)
+            def _():
+                w_copy(j, z + distance, 0).start()
+
+            w_copy(j, z + distance, 2).start()
+
+    def x_near(i, yy):
+        return remote(
+            x_out.at[i, yy], x_all.at[i, y, x], x_send.at[i, yy, 0], x_recv.at[i, y, x], at(z, yy, c, x)
+        )
+
+    def x_far(i, yy):
+        return remote(
+            x_out.at[i, yy], x_all.at[i, y, x], x_send.at[i, yy, 1], x_recv.at[i, y, x],
+            at(z, yy, c, 1 - x),
+        )
+
+    causal = (
+        lax.broadcasted_iota(jnp.int32, (tok, tok), 0) >= lax.broadcasted_iota(jnp.int32, (tok, tok), 1)
+    )
+    ms[x] = jnp.zeros(ms.shape[1:], F32)
+
+    def attend(i):
+        for yy in range(2):
+            q, k, v = (ref[:, columns(i, yy)] for ref in (q_ref, k_ref, v_ref))
+            total = jnp.zeros((tok, width), F32)
+            for h in range(group_heads):
+                scores = lax.dot_general(
+                    q * in_head16[h], k, (((1,), (1,)), ((), ())), preferred_element_type=F32
+                )
+                scores = jnp.where(causal, scores, 0.0).astype(BF16)
+                total = total + jnp.dot(scores, v * in_head16[h], preferred_element_type=F32)
+            att[...] = total
+
+            @pl.when(x == 1)
+            def _():
+                state_copy(i, yy).wait_recv()
+                state = state_in[i, yy]
+                wide = jnp.concatenate([state * m for m in in_head16], axis=0)
+                att[...] += jnp.dot(q, wide, preferred_element_type=F32)
+
+            attn = att[...]
+            ms[x] += jnp.broadcast_to(
+                jnp.sum(attn * attn, axis=-1, keepdims=True) * (1.0 / features), ms.shape[1:]
+            )
+            scaled = (attn * gain_ref[:, columns(i, yy)]).astype(BF16)
+            x_out[i, yy] = scaled
+            x_far(i, yy).start()
+
+            @pl.when(y != yy)
+            def _():
+                x_near(i, yy).start()
+
+            @pl.when(y == yy)
+            def _():
+                x_all[i, y, x] = scaled
+
+        pass_on(i, 1)
+
+    each(attend)
+    ms_copy = remote(ms.at[x], ms.at[x], ms_send, ms_recv, across)
+    ms_copy.start()
+
+    for distance in range(2, planes - 1):
+        each(functools.partial(pass_on, distance=distance))
+
+    def x_arrive(i, yy, xx):
+        remote(
+            x_all.at[i, yy, xx], x_all.at[i, yy, xx], x_send.at[i, yy, 1], x_recv.at[i, yy, xx], across
+        ).wait_recv()
+
+    def merge(i):
+        x_arrive(i, y, 1 - x)
+        x_arrive(i, 1 - y, x)
+        x_arrive(i, 1 - y, 1 - x)
+        parts = [x_all[i, yy, xx].astype(F32) for yy in range(2) for xx in range(2)]
+        x_cat[i] = jnp.concatenate(parts, axis=0).astype(BF16)
+
+    each(merge)
+
+    def multiply(j, plane):
+        w_arrive(j, plane, 1 - c)
+        return jnp.dot(
+            x_cat[plane], w_all[j, plane].reshape(width, chunk), preferred_element_type=F32
+        )
+
+    def first(j):
+        total = multiply(j, z)
+        acc[j, 0] = total[:2 * tok]
+        acc[j, 1] = total[2 * tok:]
+
+    each(first)
+
+    def add(j, plane):
+        total = multiply(j, plane)
+        acc[j, 0] += total[:2 * tok]
+        acc[j, 1] += total[2 * tok:]
+
+    def add_both(j, distance):
+        @pl.when(z - distance >= 0)
+        def _():
+            add(j, z - distance)
+
+        @pl.when(z + distance < planes)
+        def _():
+            add(j, z + distance)
+
+    for distance in range(1, planes - 1):
+        each(functools.partial(add_both, distance=distance))
+
+    def part_copy(j):
+        return remote(part_out.at[j], part_in.at[j], part_send.at[j], part_recv.at[j], beside)
+
+    def last(j):
+        pass_on(j, planes - 1)
+        add_both(j, planes - 1)
+        part_out[j] = acc[j, 1 - y].astype(BF16)
+        part_copy(j).start()
+
+    each(last)
+
+    remote(ms.at[1 - x], ms.at[1 - x], ms_send, ms_recv, across).wait_recv()
+    mean_sq = jnp.concatenate([ms[0][:, :1], ms[1][:, :1]], axis=0)
+    scale = lax.rsqrt(mean_sq + 1e-05)
+
+    def finish(j):
+        part_copy(j).wait_recv()
+        total = acc[j, y] + part_in[j].astype(F32)
+        out_ref[:, pl.ds(pl.multiple_of(j * chunk, chunk), chunk)] = (total * scale).astype(BF16)
+
+    each(finish)
+
+    def drain(i):
+        part_copy(i).wait_send()
+        for yy in range(2):
+            x_far(i, yy).wait_send()
+
+            @pl.when(y != yy)
+            def _():
+                x_near(i, yy).wait_send()
+
+            @pl.when(x == 0)
+            def _():
+                state_copy(i, yy).wait_send()
+
+        for plane in range(planes):
+            w_copy(i, plane, 2).wait_send()
+
+            @pl.when((plane >= z) & (z > 0))
+            def _():
+                w_copy(i, plane, 0).wait_send()
+
+            @pl.when((plane <= z) & (z < planes - 1))
+            def _():
+                w_copy(i, plane, 1).wait_send()
+
+    each(drain)
+    ms_copy.wait_send()
+
+
+def fused(planes, queries, keys, values, norm_gain, out_weight):
+    tok, features = queries.shape
+    rows, out_columns = out_weight.shape
+    width, chunk = 2 * rows, out_columns // planes
+    vmem = pl.BlockSpec(memory_space=pltpu.VMEM)
+    dma = pltpu.SemaphoreType.DMA
+    return pl.pallas_call(
+        functools.partial(kernel, planes),
+        out_shape=jax.ShapeDtypeStruct((2 * tok, out_columns), BF16),
+        in_specs=[vmem, vmem, vmem, vmem, pl.BlockSpec(memory_space=pl.ANY)],
+        out_specs=vmem,
+        scratch_shapes=[
+            pltpu.VMEM((planes, planes, 2, rows, chunk), BF16),
+            pltpu.VMEM((planes, 2, HEAD_DIM, width), BF16),
+            pltpu.VMEM((planes, 2, HEAD_DIM, width), BF16),
+            pltpu.VMEM((planes, 2, tok, width), BF16),
+            pltpu.VMEM((planes, 2, 2, tok, width), BF16),
+            pltpu.VMEM((planes, 4 * tok, width), BF16),
+            pltpu.VMEM((tok, width), F32),
+            pltpu.VMEM((2, tok, 128), F32),
+            pltpu.VMEM((planes, 2, 2 * tok, chunk), F32),
+            pltpu.VMEM((planes, 2 * tok, chunk), BF16),
+            pltpu.VMEM((planes, 2 * tok, chunk), BF16),
+            dma((planes,)),
+            dma((planes, planes, 3)),
+            dma((planes, planes, 2)),
+            dma((planes, 2)),
+            dma((planes, 2)),
+            dma((planes, 2, 2)),
+            dma((planes, 2, 2)),
+            dma,
+            dma,
+            dma((planes,)),
+            dma((planes,)),
+        ],
+        compiler_params=pltpu.CompilerParams(
+            collective_id=0, has_side_effects=True, vmem_limit_bytes=40 * 1024 * 1024
+        ),
+    )(queries, keys, values, norm_gain.reshape(1, features), out_weight)
+
+
 def solution(mesh):
     placed = (
         P(("fsdp", "ctx"), None),
@@ -44,6 +379,24 @@
         P(),
         P("fsdp", "ctx"),
     )
+    planes = mesh.shape["fsdp"] // 4
+
+    def body(queries, keys, values, norm_gain, out_weight):
+        rows, out_columns = out_weight.shape
+        width = 2 * rows
+        fits = (
+            mesh.shape["ctx"] == 2
+            and mesh.shape["fsdp"] == 4 * planes
+            and 3 <= planes <= 4
+            and rows % 16 == 0
+            and width % HEAD_DIM == 0
+            and width % 128 == 0
+            and out_columns % (128 * planes) == 0
+        )
+        if fits:
+            return fused(planes, queries, keys, values, norm_gain, out_weight)
+        return on_device(queries, keys, values, norm_gain, out_weight)
+
     return jax.shard_map(
-        on_device, mesh=mesh, in_specs=placed, out_specs=P("fsdp", "ctx"), check_vma=False
+        body, mesh=mesh, in_specs=placed, out_specs=P("fsdp", "ctx"), check_vma=False
     )

time: 168 us -> 60.3 us (0.36)
  waiting for transfers between devices: 131 us -> 0 us
  Pallas kernels: 0 us -> 54.1 us
  between operations: 13.2 us -> 0.01 us
  matrix products: 11.8 us -> 0 us
  other arithmetic: 3.69 us -> 0 us
  local copies, waits for them, and re-layouts: 7.85 us -> 5.85 us
    all_gather x3 -> x0, waiting for transfers between devices: 130 us -> none  [the longest x1 83.8 us: on_device(): weight_block = lax.all_gather(out_weight, 'fsdp', axis=0, tiled=True)]
    pallas_call x0 -> x1, Pallas kernels: none -> 54.1 us  [fused(): pl.pallas_call(functools.partial(kernel, planes), out_shape=jax.ShapeDtyp...]
    dot_general x4 -> x0, matrix products: 11.8 us -> none  [the longest x1 7.07 us: on_device(): jnp.dot(lax.all_gather(normed, 'ctx', axis=0, tiled=True), weight_block,...]
    unnamed x8 -> x11, local copies, waits for them, and re-layouts: 0.02 us -> 5.85 us
    reshape x4 -> x0, local copies, waits for them, and re-layouts: 4.14 us -> none  [the longest x1 1.88 us: on_device(): attn = (intra + inter).reshape(tok_rows, HEADS * HEAD_DIM)]
    convert_element_type x2 -> x0, local copies, waits for them, and re-layouts: 3.68 us -> none  [the longest x1 1.87 us: on_device(): local_state.reshape(HEADS, HEAD_DIM * HEAD_DIM).astype(jnp.bfloat16)]
    reduce_sum x1 -> x0, other arithmetic: 2.64 us -> none  [on_device(): jnp.sum(jnp.where(earlier, every_state.astype(jnp.float32), 0.0), axis=0)]
  transfers between devices with their start and end apart: 3 -> 0, of which waited for: 3 -> 0; matrix products, arithmetic and copies ran while one was open for 2% -> 0% of each run, Pallas kernels for 0% -> 0%
where the time goes in v1:
time: 60.3 us; the launch traced here: 60 us
  Pallas kernels  54.1 us (90%)
  local copies, waits for them, and re-layouts  5.85 us (10%)
    pallas_call x1, Pallas kernels, fused(): pl.pallas_call(functools.partial(kernel, planes), out_shape=jax.ShapeDtyp...  54.1 us
    unnamed x11, local copies, waits for them, and re-layouts  5.85 us

profile of v1, /device:TPU:0, one launch (start us, length us, event | category | flops | bytes accessed | tf_op | source)
XLA Modules:
  0.0 60.0 jit_solution(1660071193628419445)
XLA Ops:
  0.0 0.0 copy-start
  0.0 1.1 %copy-done = bf16[104,3072]{1,0:T(8,128)(2,1)S(1)} copy-done((bf16[104,3072]{1,0:T(8,128)(2,1)S(1)}, bf16[104,3072]{1,0:T(8,128)(2,1)}, u32[]{:S(2)}) %copy-start) | copy-done | bytes 639000
  1.1 0.0 copy-start.1
  1.1 1.1 %copy-done.1 = bf16[104,3072]{1,0:T(8,128)(2,1)S(1)} copy-done((bf16[104,3072]{1,0:T(8,128)(2,1)S(1)}, bf16[104,3072]{1,0:T(8,128)(2,1)}, u32[]{:S(2)}) %copy-start.1) | copy-done | bytes 639000
  2.2 0.0 copy-start.2
  2.2 1.1 %copy-done.2 = bf16[104,3072]{1,0:T(8,128)(2,1)S(1)} copy-done((bf16[104,3072]{1,0:T(8,128)(2,1)S(1)}, bf16[104,3072]{1,0:T(8,128)(2,1)}, u32[]{:S(2)}) %copy-start.2) | copy-done | bytes 639000
  3.2 0.0 copy-start.3
  3.2 1.1 %copy-done.3 = bf16[192,1536]{1,0:T(8,128)(2,1)S(1)} copy-done((bf16[192,1536]{1,0:T(8,128)(2,1)S(1)}, bf16[192,1536]{1,0:T(8,128)(2,1)}, u32[]{:S(2)}) %copy-start.3) | copy-done | bytes 589848
  4.3 0.0 copy-start.4
  4.3 0.7 %copy-done.4 = f32[3072]{0:T(1024)S(1)} copy-done((f32[3072]{0:T(1024)S(1)}, f32[3072]{0:T(1024)}, u32[]{:S(2)}) %copy-start.4) | copy-done | bytes 12312
  5.0 54.1 %shard_map.55 = bf16[208,1536]{1,0:T(8,128)(2,1)S(1)} custom-call(bf16[104,3072]{1,0:T(8,128)(2,1)S(1)} %copy-done, bf16[104,3072]{1,0:T(8,128)(2,1)S(1)} %copy-done.1, bf16[104,3072]{1,0:T(8,128)(2,1)S(1)} %copy-done.2, f32[1,3072]{1,0:T(1,128)S(1)} %bitcast.1, bf16[192,1536]{1,0:T(8,128)(2,1)S(1)} %copy-done.3), custom_call_target="tpu_custom_call" | custom-call | tf_op jit(solution)/shard_map/pallas_call | solution.py:339
  59.1 0.8 %copy.7 = bf16[208,1536]{1,0:T(8,128)(2,1)} copy(bf16[208,1536]{1,0:T(8,128)(2,1)S(1)} %shard_map.55) | data formatting | bytes 1277952
Async XLA Ops:
  0.0 1.1 %copy-start = (bf16[104,3072]{1,0:T(8,128)(2,1)S(1)}, bf16[104,3072]{1,0:T(8,128)(2,1)}, u32[]{:S(2)}) copy-start(bf16[104,3072]{1,0:T(8,128)(2,1)} %q_ref.1) | copy-start | bytes 1916932
  1.1 1.1 %copy-start.1 = (bf16[104,3072]{1,0:T(8,128)(2,1)S(1)}, bf16[104,3072]{1,0:T(8,128)(2,1)}, u32[]{:S(2)}) copy-start(bf16[104,3072]{1,0:T(8,128)(2,1)} %k_ref.1) | copy-start | bytes 1916932
  2.2 1.1 %copy-start.2 = (bf16[104,3072]{1,0:T(8,128)(2,1)S(1)}, bf16[104,3072]{1,0:T(8,128)(2,1)}, u32[]{:S(2)}) copy-start(bf16[104,3072]{1,0:T(8,128)(2,1)} %v_ref.1) | copy-start | bytes 1916932
  3.2 1.1 %copy-start.3 = (bf16[192,1536]{1,0:T(8,128)(2,1)S(1)}, bf16[192,1536]{1,0:T(8,128)(2,1)}, u32[]{:S(2)}) copy-start(bf16[192,1536]{1,0:T(8,128)(2,1)} %w_ref.1) | copy-start | bytes 1769476
  4.3 0.7 %copy-start.4 = (f32[3072]{0:T(1024)S(1)}, f32[3072]{0:T(1024)}, u32[]{:S(2)}) copy-start(f32[3072]{0:T(1024)} %param.8) | copy-start | bytes 36868

commit v2 on v1

--- a/solution.py
+++ b/solution.py
@@ -44,15 +44,15 @@
 
 
 def kernel(
-    planes, q_ref, k_ref, v_ref, gain_ref, w_ref, out_ref,
-    w_all, state_own, state_in, x_out, x_all, x_cat, att, ms, acc, part_out, part_in,
+    planes, chunks, q_in, k_in, v_in, gain_in, w_ref, out_ref,
+    q_ref, k_ref, v_ref, gain_ref, w_all, out_all, state_own, state_in, x_out, x_all, x_cat, att, ms, acc, part_out, part_in,
     w_load, w_send, w_recv, state_send, state_recv, x_send, x_recv, ms_send, ms_recv,
-    part_send, part_recv,
+    part_send, part_recv, in_load, out_store,
 ):
     tok, features = q_ref.shape
     rows = w_ref.shape[0]
     width = 2 * rows
-    chunk = w_ref.shape[1] // planes
+    chunk = w_ref.shape[1] // chunks
     group_heads = width // HEAD_DIM
 
     f = lax.axis_index("fsdp")
@@ -88,13 +88,22 @@
         block = w_all.at[j, plane, core]
         remote(block, block, w_send.at[j, plane, 2], w_recv.at[j, plane, core], sibling).wait_recv()
 
-    def each(body):
+    def each(body, count=planes):
         def step(i, carry):
             body(i)
             return carry
-        lax.fori_loop(0, planes, step, 0)
-
-    each(lambda j: load(j).start())
+        lax.fori_loop(0, count, step, 0)
+
+    every_chunk = functools.partial(each, count=chunks)
+    every_chunk(lambda j: load(j).start())
+    inputs = [
+        pltpu.make_async_copy(src, dst, in_load.at[n])
+        for n, (src, dst) in enumerate(
+            ((k_in, k_ref), (v_in, v_ref), (q_in, q_ref), (gain_in, gain_ref))
+        )
+    ]
+    for copy in inputs:
+        copy.start()
 
     barrier = pltpu.get_barrier_semaphore()
     for device in (sibling, across, beside, diagonal):
@@ -123,7 +132,9 @@
 
         w_copy(j, z, 2).start()
 
-    each(send_own)
+    every_chunk(send_own)
+    for copy in inputs:
+        copy.wait()
 
     lane = lax.broadcasted_iota(jnp.int32, (1, width), 1)
     in_head = [
@@ -192,6 +203,26 @@
     )
     ms[x] = jnp.zeros(ms.shape[1:], F32)
 
+    def pass_on_share(i, distance):
+        share = chunks // planes
+        each(lambda n: pass_on(i * share + n, distance), share)
+
+    def deliver(i, yy, attn):
+        ms[x] += jnp.broadcast_to(
+            jnp.sum(attn * attn, axis=-1, keepdims=True) * (1.0 / features), ms.shape[1:]
+        )
+        scaled = (attn * gain_ref[:, columns(i, yy)]).astype(BF16)
+        x_out[i, yy] = scaled
+        x_far(i, yy).start()
+
+        @pl.when(y != yy)
+        def _():
+            x_near(i, yy).start()
+
+        @pl.when(y == yy)
+        def _():
+            x_all[i, y, x] = scaled
+
     def attend(i):
         for yy in range(2):
             q, k, v = (ref[:, columns(i, yy)] for ref in (q_ref, k_ref, v_ref))
@@ -202,39 +233,31 @@
                 )
                 scores = jnp.where(causal, scores, 0.0).astype(BF16)
                 total = total + jnp.dot(scores, v * in_head16[h], preferred_element_type=F32)
-            att[...] = total
-
-            @pl.when(x == 1)
-            def _():
+            att[i, yy] = total
+
+            @pl.when(x == 0)
+            def _():
+                deliver(i, yy, att[i, yy])
+
+        pass_on_share(i, 1)
+
+    each(attend)
+
+    def attend_earlier(i):
+        @pl.when(x == 1)
+        def _():
+            for yy in range(2):
                 state_copy(i, yy).wait_recv()
                 state = state_in[i, yy]
                 wide = jnp.concatenate([state * m for m in in_head16], axis=0)
-                att[...] += jnp.dot(q, wide, preferred_element_type=F32)
-
-            attn = att[...]
-            ms[x] += jnp.broadcast_to(
-                jnp.sum(attn * attn, axis=-1, keepdims=True) * (1.0 / features), ms.shape[1:]
-            )
-            scaled = (attn * gain_ref[:, columns(i, yy)]).astype(BF16)
-            x_out[i, yy] = scaled
-            x_far(i, yy).start()
-
-            @pl.when(y != yy)
-            def _():
-                x_near(i, yy).start()
-
-            @pl.when(y == yy)
-            def _():
-                x_all[i, y, x] = scaled
-
-        pass_on(i, 1)
-
-    each(attend)
+                inter = jnp.dot(q_ref[:, columns(i, yy)], wide, preferred_element_type=F32)
+                deliver(i, yy, att[i, yy] + inter)
+
+        pass_on_share(i, 2)
+
+    each(attend_earlier)
     ms_copy = remote(ms.at[x], ms.at[x], ms_send, ms_recv, across)
     ms_copy.start()
-
-    for distance in range(2, planes - 1):
-        each(functools.partial(pass_on, distance=distance))
 
     def x_arrive(i, yy, xx):
         remote(
@@ -261,7 +284,7 @@
         acc[j, 0] = total[:2 * tok]
         acc[j, 1] = total[2 * tok:]
 
-    each(first)
+    every_chunk(first)
 
     def add(j, plane):
         total = multiply(j, plane)
@@ -278,7 +301,7 @@
             add(j, z + distance)
 
     for distance in range(1, planes - 1):
-        each(functools.partial(add_both, distance=distance))
+        every_chunk(functools.partial(add_both, distance=distance))
 
     def part_copy(j):
         return remote(part_out.at[j], part_in.at[j], part_send.at[j], part_recv.at[j], beside)
@@ -289,21 +312,27 @@
         part_out[j] = acc[j, 1 - y].astype(BF16)
         part_copy(j).start()
 
-    each(last)
+    every_chunk(last)
 
     remote(ms.at[1 - x], ms.at[1 - x], ms_send, ms_recv, across).wait_recv()
     mean_sq = jnp.concatenate([ms[0][:, :1], ms[1][:, :1]], axis=0)
     scale = lax.rsqrt(mean_sq + 1e-05)
 
+    def store(j):
+        return pltpu.make_async_copy(
+            out_all.at[j],
+            out_ref.at[:, pl.ds(pl.multiple_of(j * chunk, chunk), chunk)], out_store.at[j],
+        )
+
     def finish(j):
         part_copy(j).wait_recv()
         total = acc[j, y] + part_in[j].astype(F32)
-        out_ref[:, pl.ds(pl.multiple_of(j * chunk, chunk), chunk)] = (total * scale).astype(BF16)
-
-    each(finish)
+        out_all[j] = (total * scale).astype(BF16)
+        store(j).start()
+
+    every_chunk(finish)
 
     def drain(i):
-        part_copy(i).wait_send()
         for yy in range(2):
             x_far(i, yy).wait_send()
 
@@ -315,6 +344,10 @@
             def _():
                 state_copy(i, yy).wait_send()
 
+    def drain_chunk(i):
+        part_copy(i).wait_send()
+        store(i).wait()
+
         for plane in range(planes):
             w_copy(i, plane, 2).wait_send()
 
@@ -327,46 +360,54 @@
                 w_copy(i, plane, 1).wait_send()
 
     each(drain)
+    every_chunk(drain_chunk)
     ms_copy.wait_send()
 
 
-def fused(planes, queries, keys, values, norm_gain, out_weight):
+def fused(planes, chunks, queries, keys, values, norm_gain, out_weight):
     tok, features = queries.shape
     rows, out_columns = out_weight.shape
-    width, chunk = 2 * rows, out_columns // planes
-    vmem = pl.BlockSpec(memory_space=pltpu.VMEM)
+    width, chunk = 2 * rows, out_columns // chunks
+    anywhere = pl.BlockSpec(memory_space=pl.ANY)
     dma = pltpu.SemaphoreType.DMA
     return pl.pallas_call(
-        functools.partial(kernel, planes),
+        functools.partial(kernel, planes, chunks),
         out_shape=jax.ShapeDtypeStruct((2 * tok, out_columns), BF16),
-        in_specs=[vmem, vmem, vmem, vmem, pl.BlockSpec(memory_space=pl.ANY)],
-        out_specs=vmem,
+        in_specs=[anywhere] * 5,
+        out_specs=anywhere,
         scratch_shapes=[
-            pltpu.VMEM((planes, planes, 2, rows, chunk), BF16),
+            pltpu.VMEM((tok, features), BF16),
+            pltpu.VMEM((tok, features), BF16),
+            pltpu.VMEM((tok, features), BF16),
+            pltpu.VMEM((1, features), F32),
+            pltpu.VMEM((chunks, planes, 2, rows, chunk), BF16),
+            pltpu.VMEM((chunks, 2 * tok, chunk), BF16),
             pltpu.VMEM((planes, 2, HEAD_DIM, width), BF16),
             pltpu.VMEM((planes, 2, HEAD_DIM, width), BF16),
             pltpu.VMEM((planes, 2, tok, width), BF16),
             pltpu.VMEM((planes, 2, 2, tok, width), BF16),
             pltpu.VMEM((planes, 4 * tok, width), BF16),
-            pltpu.VMEM((tok, width), F32),
+            pltpu.VMEM((planes, 2, tok, width), F32),
             pltpu.VMEM((2, tok, 128), F32),
-            pltpu.VMEM((planes, 2, 2 * tok, chunk), F32),
-            pltpu.VMEM((planes, 2 * tok, chunk), BF16),
-            pltpu.VMEM((planes, 2 * tok, chunk), BF16),
-            dma((planes,)),
-            dma((planes, planes, 3)),
-            dma((planes, planes, 2)),
+            pltpu.VMEM((chunks, 2, 2 * tok, chunk), F32),
+            pltpu.VMEM((chunks, 2 * tok, chunk), BF16),
+            pltpu.VMEM((chunks, 2 * tok, chunk), BF16),
+            dma((chunks,)),
+            dma((chunks, planes, 3)),
+            dma((chunks, planes, 2)),
             dma((planes, 2)),
             dma((planes, 2)),
             dma((planes, 2, 2)),
             dma((planes, 2, 2)),
             dma,
             dma,
-            dma((planes,)),
-            dma((planes,)),
+            dma((chunks,)),
+            dma((chunks,)),
+            dma((4,)),
+            dma((chunks,)),
         ],
         compiler_params=pltpu.CompilerParams(
-            collective_id=0, has_side_effects=True, vmem_limit_bytes=40 * 1024 * 1024
+            collective_id=0, has_side_effects=True, vmem_limit_bytes=56 * 1024 * 1024
         ),
     )(queries, keys, values, norm_gain.reshape(1, features), out_weight)
 
@@ -380,6 +421,7 @@
         P("fsdp", "ctx"),
     )
     planes = mesh.shape["fsdp"] // 4
+    chunks = planes
 
     def body(queries, keys, values, norm_gain, out_weight):
         rows, out_columns = out_weight.shape
@@ -387,14 +429,14 @@
         fits = (
             mesh.shape["ctx"] == 2
             and mesh.shape["fsdp"] == 4 * planes
-            and 3 <= planes <= 4
+            and planes == 4
             and rows % 16 == 0
             and width % HEAD_DIM == 0
             and width % 128 == 0
-            and out_columns % (128 * planes) == 0
+            and out_columns % (128 * chunks) == 0
         )
         if fits:
-            return fused(planes, queries, keys, values, norm_gain, out_weight)
+            return fused(planes, chunks, queries, keys, values, norm_gain, out_weight)
         return on_device(queries, keys, values, norm_gain, out_weight)
 
     return jax.shard_map(

time: 60.3 us -> 59.9 us (level)
  local copies, waits for them, and re-layouts: 5.85 us -> 1.95 us
  Pallas kernels: 54.1 us -> 57.7 us
    unnamed x11 -> x1, local copies, waits for them, and re-layouts: 5.85 us -> 1.95 us
    pallas_call x1, Pallas kernels: 54.1 us -> 57.7 us  [fused(): pl.pallas_call(functools.partial(kernel, planes, chunks), out_shape=jax.S...]
where the time goes in v2:
time: 59.9 us; the launch traced here: 59.7 us
  Pallas kernels  57.7 us (96%)
  local copies, waits for them, and re-layouts  1.95 us (3%)
    pallas_call x1, Pallas kernels, fused(): pl.pallas_call(functools.partial(kernel, planes, chunks), out_shape=jax.S...  57.7 us
    unnamed x1, local copies, waits for them, and re-layouts  1.95 us

profile of v2, /device:TPU:0, one launch (start us, length us, event | category | flops | bytes accessed | tf_op | source)
XLA Modules:
  0.0 59.7 jit_solution(11437902163326472260)
XLA Ops:
  0.0 57.7 %shard_map.55 = bf16[208,1536]{1,0:T(8,128)(2,1)} custom-call(bf16[104,3072]{1,0:T(8,128)(2,1)} %q_in.1, bf16[104,3072]{1,0:T(8,128)(2,1)} %k_in.1, bf16[104,3072]{1,0:T(8,128)(2,1)} %v_in.1, f32[1,3072]{1,0:T(1,128)} %bitcast.1, bf16[192,1536]{1,0:T(8,128)(2,1)} %w_ref.1), custom_call_target="tpu_custom_call" | custom-call | tf_op jit(solution)/shard_map/pallas_call | solution.py:373
  57.8 2.0 %copy.7 = bf16[208,1536]{1,0:T(8,128)(2,1)} copy(bf16[208,1536]{1,0:T(8,128)(2,1)} %shard_map.55) | data formatting | bytes 1277952

commit v3 on v2

--- a/solution.py
+++ b/solution.py
@@ -45,9 +45,9 @@
 
 def kernel(
     planes, chunks, q_in, k_in, v_in, gain_in, w_ref, out_ref,
-    q_ref, k_ref, v_ref, gain_ref, w_all, out_all, state_own, state_in, x_out, x_all, x_cat, att, ms, acc, part_out, part_in,
+    q_ref, k_ref, v_ref, gain_ref, w_all, state_own, state_in, x_out, x_all, x_cat, att, ms, acc, part_out, part_in,
     w_load, w_send, w_recv, state_send, state_recv, x_send, x_recv, ms_send, ms_recv,
-    part_send, part_recv, in_load, out_store,
+    part_send, part_recv, in_load,
 ):
     tok, features = q_ref.shape
     rows = w_ref.shape[0]
@@ -63,6 +63,8 @@
         return (4 * zz + 2 * yy + cc, xx)
 
     sibling = at(z, y, 1 - c, x)
+    far_end = at(planes - 1 - z, y, c, x)
+    at_end = (z == 0) | (z == planes - 1)
     across = at(z, y, c, 1 - x)
     beside = at(z, 1 - y, c, x)
     diagonal = at(z, 1 - y, c, 1 - x)
@@ -80,7 +82,7 @@
         )
 
     def w_copy(j, plane, way):
-        device = (at(z - 1, y, c, x), at(z + 1, y, c, x), sibling)[way]
+        device = (at(z - 1, y, c, x), at(z + 1, y, c, x), sibling, far_end)[way]
         block = w_all.at[j, plane, c]
         return remote(block, block, w_send.at[j, plane, way], w_recv.at[j, plane, c], device)
 
@@ -117,7 +119,11 @@
     def _():
         pl.semaphore_signal(barrier, inc=1, device_id=at(z + 1, y, c, x), device_id_type=MESH)
 
-    pl.semaphore_wait(barrier, 4 + jnp.where(z > 0, 1, 0) + jnp.where(z < planes - 1, 1, 0))
+    @pl.when(at_end)
+    def _():
+        pl.semaphore_signal(barrier, inc=1, device_id=far_end, device_id_type=MESH)
+
+    pl.semaphore_wait(barrier, 4 + jnp.where(at_end, 1, 0) + jnp.where(z > 0, 1, 0) + jnp.where(z < planes - 1, 1, 0))
 
     def send_own(j):
         load(j).wait()
@@ -131,6 +137,10 @@
             w_copy(j, z, 1).start()
 
         w_copy(j, z, 2).start()
+
+        @pl.when(at_end)
+        def _():
+            w_copy(j, z, 3).start()
 
     every_chunk(send_own)
     for copy in inputs:
@@ -170,20 +180,20 @@
         @pl.when(z - distance >= 0)
         def _():
             w_arrive(j, z - distance, c)
-
-            @pl.when(z < planes - 1)
-            def _():
-                w_copy(j, z - distance, 1).start()
+            if distance == 1:
+                @pl.when(z < planes - 1)
+                def _():
+                    w_copy(j, z - 1, 1).start()
 
             w_copy(j, z - distance, 2).start()
 
         @pl.when(z + distance < planes)
         def _():
             w_arrive(j, z + distance, c)
-
-            @pl.when(z > 0)
-            def _():
-                w_copy(j, z + distance, 0).start()
+            if distance == 1:
+                @pl.when(z > 0)
+                def _():
+                    w_copy(j, z + 1, 0).start()
 
             w_copy(j, z + distance, 2).start()
 
@@ -202,10 +212,6 @@
         lax.broadcasted_iota(jnp.int32, (tok, tok), 0) >= lax.broadcasted_iota(jnp.int32, (tok, tok), 1)
     )
     ms[x] = jnp.zeros(ms.shape[1:], F32)
-
-    def pass_on_share(i, distance):
-        share = chunks // planes
-        each(lambda n: pass_on(i * share + n, distance), share)
 
     def deliver(i, yy, attn):
         ms[x] += jnp.broadcast_to(
@@ -239,9 +245,11 @@
             def _():
                 deliver(i, yy, att[i, yy])
 
-        pass_on_share(i, 1)
+        pass_on(i, 1)
 
     each(attend)
+    for j in range(planes, chunks):
+        pass_on(j, 1)
 
     def attend_earlier(i):
         @pl.when(x == 1)
@@ -253,8 +261,6 @@
                 inter = jnp.dot(q_ref[:, columns(i, yy)], wide, preferred_element_type=F32)
                 deliver(i, yy, att[i, yy] + inter)
 
-        pass_on_share(i, 2)
-
     each(attend_earlier)
     ms_copy = remote(ms.at[x], ms.at[x], ms_send, ms_recv, across)
     ms_copy.start()
@@ -300,15 +306,16 @@
         def _():
             add(j, z + distance)
 
-    for distance in range(1, planes - 1):
-        every_chunk(functools.partial(add_both, distance=distance))
+    every_chunk(functools.partial(add_both, distance=1))
 
     def part_copy(j):
         return remote(part_out.at[j], part_in.at[j], part_send.at[j], part_recv.at[j], beside)
 
     def last(j):
-        pass_on(j, planes - 1)
-        add_both(j, planes - 1)
+        for distance in range(2, planes):
+            pass_on(j, distance)
+        for distance in range(2, planes):
+            add_both(j, distance)
         part_out[j] = acc[j, 1 - y].astype(BF16)
         part_copy(j).start()
 
@@ -318,17 +325,10 @@
     mean_sq = jnp.concatenate([ms[0][:, :1], ms[1][:, :1]], axis=0)
     scale = lax.rsqrt(mean_sq + 1e-05)
 
-    def store(j):
-        return pltpu.make_async_copy(
-            out_all.at[j],
-            out_ref.at[:, pl.ds(pl.multiple_of(j * chunk, chunk), chunk)], out_store.at[j],
-        )
-
     def finish(j):
         part_copy(j).wait_recv()
         total = acc[j, y] + part_in[j].astype(F32)
-        out_all[j] = (total * scale).astype(BF16)
-        store(j).start()
+        out_ref[:, pl.ds(pl.multiple_of(j * chunk, chunk), chunk)] = (total * scale).astype(BF16)
 
     every_chunk(finish)
 
@@ -346,18 +346,21 @@
 
     def drain_chunk(i):
         part_copy(i).wait_send()
-        store(i).wait()
 
         for plane in range(planes):
             w_copy(i, plane, 2).wait_send()
 
-            @pl.when((plane >= z) & (z > 0))
+            @pl.when(((plane == z) | (plane == z + 1)) & (z > 0))
             def _():
                 w_copy(i, plane, 0).wait_send()
 
-            @pl.when((plane <= z) & (z < planes - 1))
+            @pl.when(((plane == z) | (plane == z - 1)) & (z < planes - 1))
             def _():
                 w_copy(i, plane, 1).wait_send()
+
+        @pl.when(at_end)
+        def _():
+            w_copy(i, z, 3).wait_send()
 
     each(drain)
     every_chunk(drain_chunk)
@@ -374,14 +377,13 @@
         functools.partial(kernel, planes, chunks),
         out_shape=jax.ShapeDtypeStruct((2 * tok, out_columns), BF16),
         in_specs=[anywhere] * 5,
-        out_specs=anywhere,
+        out_specs=pl.BlockSpec(memory_space=pltpu.VMEM),
         scratch_shapes=[
             pltpu.VMEM((tok, features), BF16),
             pltpu.VMEM((tok, features), BF16),
             pltpu.VMEM((tok, features), BF16),
             pltpu.VMEM((1, features), F32),
             pltpu.VMEM((chunks, planes, 2, rows, chunk), BF16),
-            pltpu.VMEM((chunks, 2 * tok, chunk), BF16),
             pltpu.VMEM((planes, 2, HEAD_DIM, width), BF16),
             pltpu.VMEM((planes, 2, HEAD_DIM, width), BF16),
             pltpu.VMEM((planes, 2, tok, width), BF16),
@@ -393,7 +395,7 @@
             pltpu.VMEM((chunks, 2 * tok, chunk), BF16),
             pltpu.VMEM((chunks, 2 * tok, chunk), BF16),
             dma((chunks,)),
-            dma((chunks, planes, 3)),
+            dma((chunks, planes, 4)),
             dma((chunks, planes, 2)),
             dma((planes, 2)),
             dma((planes, 2)),
@@ -404,10 +406,9 @@
             dma((chunks,)),
             dma((chunks,)),
             dma((4,)),
-            dma((chunks,)),
         ],
         compiler_params=pltpu.CompilerParams(
-            collective_id=0, has_side_effects=True, vmem_limit_bytes=56 * 1024 * 1024
+            collective_id=0, has_side_effects=True, vmem_limit_bytes=48 * 1024 * 1024
         ),
     )(queries, keys, values, norm_gain.reshape(1, features), out_weight)
 
@@ -421,7 +422,7 @@
         P("fsdp", "ctx"),
     )
     planes = mesh.shape["fsdp"] // 4
-    chunks = planes
+    chunks = 6
 
     def body(queries, keys, values, norm_gain, out_weight):
         rows, out_columns = out_weight.shape

time: 59.9 us -> 74.9 us (1.25)
  the two profiles are of different devices: /device:TPU:0 before, /device:TPU:9 now
where the time goes in v3:
time: 74.9 us; the launch traced here: 74.5 us
  Pallas kernels  68.7 us (92%)
  local copies, waits for them, and re-layouts  5.85 us (8%)
    pallas_call x1, Pallas kernels, fused(): pl.pallas_call(functools.partial(kernel, planes, chunks), out_shape=jax.S...  68.7 us
    unnamed x11, local copies, waits for them, and re-layouts  5.85 us

profile of v3, /device:TPU:9, one launch (start us, length us, event | category | flops | bytes accessed | tf_op | source)
XLA Modules:
  0.0 74.5 jit_solution(3769031200069784483)
XLA Ops:
  0.0 0.0 copy-start
  0.0 1.1 %copy-done = bf16[104,3072]{1,0:T(8,128)(2,1)S(1)} copy-done((bf16[104,3072]{1,0:T(8,128)(2,1)S(1)}, bf16[104,3072]{1,0:T(8,128)(2,1)}, u32[]{:S(2)}) %copy-start) | copy-done | bytes 639000
  1.1 0.0 copy-start.1
  1.1 1.1 %copy-done.1 = bf16[104,3072]{1,0:T(8,128)(2,1)S(1)} copy-done((bf16[104,3072]{1,0:T(8,128)(2,1)S(1)}, bf16[104,3072]{1,0:T(8,128)(2,1)}, u32[]{:S(2)}) %copy-start.1) | copy-done | bytes 639000
  2.2 0.0 copy-start.2
  2.2 1.1 %copy-done.2 = bf16[104,3072]{1,0:T(8,128)(2,1)S(1)} copy-done((bf16[104,3072]{1,0:T(8,128)(2,1)S(1)}, bf16[104,3072]{1,0:T(8,128)(2,1)}, u32[]{:S(2)}) %copy-start.2) | copy-done | bytes 639000
  3.2 0.0 copy-start.3
  3.2 1.1 %copy-done.3 = bf16[192,1536]{1,0:T(8,128)(2,1)S(1)} copy-done((bf16[192,1536]{1,0:T(8,128)(2,1)S(1)}, bf16[192,1536]{1,0:T(8,128)(2,1)}, u32[]{:S(2)}) %copy-start.3) | copy-done | bytes 589848
  4.3 0.0 copy-start.4
  4.3 0.7 copy-done.4
  5.0 68.7 %shard_map.55 = bf16[208,1536]{1,0:T(8,128)(2,1)S(1)} custom-call(bf16[104,3072]{1,0:T(8,128)(2,1)S(1)} %copy-done, bf16[104,3072]{1,0:T(8,128)(2,1)S(1)} %copy-done.1, bf16[104,3072]{1,0:T(8,128)(2,1)S(1)} %copy-done.2, f32[1,3072]{1,0:T(1,128)S(1)} %bitcast.1, bf16[192,1536]{1,0:T(8,128)(2,1)S(1)} %copy-done.3), custom_call_target="tpu_custom_call" | custom-call | tf_op jit(solution)/shard_map/pallas_call | solution.py:376
  73.7 0.8 %copy.7 = bf16[208,1536]{1,0:T(8,128)(2,1)} copy(bf16[208,1536]{1,0:T(8,128)(2,1)S(1)} %shard_map.55) | data formatting | bytes 1277952
Async XLA Ops:
  0.0 1.1 %copy-start = (bf16[104,3072]{1,0:T(8,128)(2,1)S(1)}, bf16[104,3072]{1,0:T(8,128)(2,1)}, u32[]{:S(2)}) copy-start(bf16[104,3072]{1,0:T(8,128)(2,1)} %q_in.1) | copy-start | bytes 1916932
  1.1 1.1 %copy-start.1 = (bf16[104,3072]{1,0:T(8,128)(2,1)S(1)}, bf16[104,3072]{1,0:T(8,128)(2,1)}, u32[]{:S(2)}) copy-start(bf16[104,3072]{1,0:T(8,128)(2,1)} %k_in.1) | copy-start | bytes 1916932
  2.2 1.1 %copy-start.2 = (bf16[104,3072]{1,0:T(8,128)(2,1)S(1)}, bf16[104,3072]{1,0:T(8,128)(2,1)}, u32[]{:S(2)}) copy-start(bf16[104,3072]{1,0:T(8,128)(2,1)} %v_in.1) | copy-start | bytes 1916932
  3.2 1.1 %copy-start.3 = (bf16[192,1536]{1,0:T(8,128)(2,1)S(1)}, bf16[192,1536]{1,0:T(8,128)(2,1)}, u32[]{:S(2)}) copy-start(bf16[192,1536]{1,0:T(8,128)(2,1)} %w_ref.1) | copy-start | bytes 1769476
  4.3 0.7 copy-start.4

commit v4 on v2

--- a/solution.py
+++ b/solution.py
@@ -45,9 +45,9 @@
 
 def kernel(
     planes, chunks, q_in, k_in, v_in, gain_in, w_ref, out_ref,
-    q_ref, k_ref, v_ref, gain_ref, w_all, out_all, state_own, state_in, x_out, x_all, x_cat, att, ms, acc, part_out, part_in,
+    q_ref, k_ref, v_ref, gain_ref, w_all, state_own, state_in, x_out, x_all, x_cat, att, ms, acc, part_out, part_in,
     w_load, w_send, w_recv, state_send, state_recv, x_send, x_recv, ms_send, ms_recv,
-    part_send, part_recv, in_load, out_store,
+    part_send, part_recv, in_load,
 ):
     tok, features = q_ref.shape
     rows = w_ref.shape[0]
@@ -203,17 +203,12 @@
     )
     ms[x] = jnp.zeros(ms.shape[1:], F32)
 
-    def pass_on_share(i, distance):
-        share = chunks // planes
-        each(lambda n: pass_on(i * share + n, distance), share)
-
     def deliver(i, yy, attn):
         ms[x] += jnp.broadcast_to(
             jnp.sum(attn * attn, axis=-1, keepdims=True) * (1.0 / features), ms.shape[1:]
         )
         scaled = (attn * gain_ref[:, columns(i, yy)]).astype(BF16)
         x_out[i, yy] = scaled
-        x_far(i, yy).start()
 
         @pl.when(y != yy)
         def _():
@@ -239,9 +234,18 @@
             def _():
                 deliver(i, yy, att[i, yy])
 
-        pass_on_share(i, 1)
+        pass_on(i, 1)
 
     each(attend)
+    for j in range(planes, chunks):
+        pass_on(j, 1)
+
+    @pl.when(x == 0)
+    def _():
+        def states_sent(i):
+            for yy in range(2):
+                state_copy(i, yy).wait_send()
+        each(states_sent)
 
     def attend_earlier(i):
         @pl.when(x == 1)
@@ -253,9 +257,13 @@
                 inter = jnp.dot(q_ref[:, columns(i, yy)], wide, preferred_element_type=F32)
                 deliver(i, yy, att[i, yy] + inter)
 
-        pass_on_share(i, 2)
+        for yy in range(2):
+            x_far(i, yy).start()
+        pass_on(i, 2)
 
     each(attend_earlier)
+    for j in range(planes, chunks):
+        pass_on(j, 2)
     ms_copy = remote(ms.at[x], ms.at[x], ms_send, ms_recv, across)
     ms_copy.start()
 
@@ -318,17 +326,10 @@
     mean_sq = jnp.concatenate([ms[0][:, :1], ms[1][:, :1]], axis=0)
     scale = lax.rsqrt(mean_sq + 1e-05)
 
-    def store(j):
-        return pltpu.make_async_copy(
-            out_all.at[j],
-            out_ref.at[:, pl.ds(pl.multiple_of(j * chunk, chunk), chunk)], out_store.at[j],
-        )
-
     def finish(j):
         part_copy(j).wait_recv()
         total = acc[j, y] + part_in[j].astype(F32)
-        out_all[j] = (total * scale).astype(BF16)
-        store(j).start()
+        out_ref[:, pl.ds(pl.multiple_of(j * chunk, chunk), chunk)] = (total * scale).astype(BF16)
 
     every_chunk(finish)
 
@@ -340,13 +341,8 @@
             def _():
                 x_near(i, yy).wait_send()
 
-            @pl.when(x == 0)
-            def _():
-                state_copy(i, yy).wait_send()
-
     def drain_chunk(i):
         part_copy(i).wait_send()
-        store(i).wait()
 
         for plane in range(planes):
             w_copy(i, plane, 2).wait_send()
@@ -374,14 +370,13 @@
         functools.partial(kernel, planes, chunks),
         out_shape=jax.ShapeDtypeStruct((2 * tok, out_columns), BF16),
         in_specs=[anywhere] * 5,
-        out_specs=anywhere,
+        out_specs=pl.BlockSpec(memory_space=pltpu.VMEM),
         scratch_shapes=[
             pltpu.VMEM((tok, features), BF16),
             pltpu.VMEM((tok, features), BF16),
             pltpu.VMEM((tok, features), BF16),
             pltpu.VMEM((1, features), F32),
             pltpu.VMEM((chunks, planes, 2, rows, chunk), BF16),
-            pltpu.VMEM((chunks, 2 * tok, chunk), BF16),
             pltpu.VMEM((planes, 2, HEAD_DIM, width), BF16),
             pltpu.VMEM((planes, 2, HEAD_DIM, width), BF16),
             pltpu.VMEM((planes, 2, tok, width), BF16),
@@ -404,7 +399,6 @@
             dma((chunks,)),
             dma((chunks,)),
             dma((4,)),
-            dma((chunks,)),
         ],
         compiler_params=pltpu.CompilerParams(
             collective_id=0, has_side_effects=True, vmem_limit_bytes=56 * 1024 * 1024
@@ -421,7 +415,7 @@
         P("fsdp", "ctx"),
     )
     planes = mesh.shape["fsdp"] // 4
-    chunks = planes
+    chunks = 6
 
     def body(queries, keys, values, norm_gain, out_weight):
         rows, out_columns = out_weight.shape

time: 59.9 us -> 61.3 us (1.023)
  Pallas kernels: 57.7 us -> 59.2 us
    pallas_call x1, Pallas kernels: 57.7 us -> 59.2 us  [fused(): pl.pallas_call(functools.partial(kernel, planes, chunks), out_shape=jax.S...]
where the time goes in v4:
time: 61.3 us; the launch traced here: 61.1 us
  Pallas kernels  59.2 us (97%)
  local copies, waits for them, and re-layouts  1.95 us (3%)
    pallas_call x1, Pallas kernels, fused(): pl.pallas_call(functools.partial(kernel, planes, chunks), out_shape=jax.S...  59.2 us
    unnamed x1, local copies, waits for them, and re-layouts  1.95 us

profile of v4, /device:TPU:0, one launch (start us, length us, event | category | flops | bytes accessed | tf_op | source)
XLA Modules:
  0.0 61.1 jit_solution(3357213555042781544)
XLA Ops:
  0.0 59.2 %shard_map.55 = bf16[208,1536]{1,0:T(8,128)(2,1)} custom-call(bf16[104,3072]{1,0:T(8,128)(2,1)} %q_in.1, bf16[104,3072]{1,0:T(8,128)(2,1)} %k_in.1, bf16[104,3072]{1,0:T(8,128)(2,1)} %v_in.1, f32[1,3072]{1,0:T(1,128)} %bitcast.1, bf16[192,1536]{1,0:T(8,128)(2,1)} %w_ref.1), custom_call_target="tpu_custom_call" | custom-call | tf_op jit(solution)/shard_map/pallas_call | solution.py:369
  59.2 2.0 %copy.7 = bf16[208,1536]{1,0:T(8,128)(2,1)} copy(bf16[208,1536]{1,0:T(8,128)(2,1)} %shard_map.55) | data formatting | bytes 1277952

commit v5 on v2

--- a/solution.py
+++ b/solution.py
@@ -45,9 +45,9 @@
 
 def kernel(
     planes, chunks, q_in, k_in, v_in, gain_in, w_ref, out_ref,
-    q_ref, k_ref, v_ref, gain_ref, w_all, out_all, state_own, state_in, x_out, x_all, x_cat, att, ms, acc, part_out, part_in,
+    q_ref, k_ref, v_ref, gain_ref, w_all, state_own, state_in, x_out, x_all, x_cat, att, ms, acc, part_out, part_in,
     w_load, w_send, w_recv, state_send, state_recv, x_send, x_recv, ms_send, ms_recv,
-    part_send, part_recv, in_load, out_store,
+    part_send, part_recv, in_load,
 ):
     tok, features = q_ref.shape
     rows = w_ref.shape[0]
@@ -129,8 +129,6 @@
         @pl.when(z < planes - 1)
         def _():
             w_copy(j, z, 1).start()
-
-        w_copy(j, z, 2).start()
 
     every_chunk(send_own)
     for copy in inputs:
@@ -175,7 +173,8 @@
             def _():
                 w_copy(j, z - distance, 1).start()
 
-            w_copy(j, z - distance, 2).start()
+            if distance > 1:
+                w_copy(j, z - distance, 2).start()
 
         @pl.when(z + distance < planes)
         def _():
@@ -185,7 +184,8 @@
             def _():
                 w_copy(j, z + distance, 0).start()
 
-            w_copy(j, z + distance, 2).start()
+            if distance > 1:
+                w_copy(j, z + distance, 2).start()
 
     def x_near(i, yy):
         return remote(
@@ -243,6 +243,17 @@
 
     each(attend)
 
+    every_chunk(lambda j: w_copy(j, z, 2).start())
+
+    def share_near(j):
+        @pl.when(z > 0)
+        def _():
+            w_copy(j, z - 1, 2).start()
+
+        @pl.when(z < planes - 1)
+        def _():
+            w_copy(j, z + 1, 2).start()
+
     def attend_earlier(i):
         @pl.when(x == 1)
         def _():
@@ -254,6 +265,7 @@
                 deliver(i, yy, att[i, yy] + inter)
 
         pass_on_share(i, 2)
+        each(lambda n: share_near(i * (chunks // planes) + n), chunks // planes)
 
     each(attend_earlier)
     ms_copy = remote(ms.at[x], ms.at[x], ms_send, ms_recv, across)
@@ -318,17 +330,10 @@
     mean_sq = jnp.concatenate([ms[0][:, :1], ms[1][:, :1]], axis=0)
     scale = lax.rsqrt(mean_sq + 1e-05)
 
-    def store(j):
-        return pltpu.make_async_copy(
-            out_all.at[j],
-            out_ref.at[:, pl.ds(pl.multiple_of(j * chunk, chunk), chunk)], out_store.at[j],
-        )
-
     def finish(j):
         part_copy(j).wait_recv()
         total = acc[j, y] + part_in[j].astype(F32)
-        out_all[j] = (total * scale).astype(BF16)
-        store(j).start()
+        out_ref[:, pl.ds(pl.multiple_of(j * chunk, chunk), chunk)] = (total * scale).astype(BF16)
 
     every_chunk(finish)
 
@@ -346,7 +351,6 @@
 
     def drain_chunk(i):
         part_copy(i).wait_send()
-        store(i).wait()
 
         for plane in range(planes):
             w_copy(i, plane, 2).wait_send()
@@ -368,20 +372,19 @@
     tok, features = queries.shape
     rows, out_columns = out_weight.shape
     width, chunk = 2 * rows, out_columns // chunks
-    anywhere = pl.BlockSpec(memory_space=pl.ANY)
+    hbm = pl.BlockSpec(memory_space=pltpu.HBM)
     dma = pltpu.SemaphoreType.DMA
     return pl.pallas_call(
         functools.partial(kernel, planes, chunks),
         out_shape=jax.ShapeDtypeStruct((2 * tok, out_columns), BF16),
-        in_specs=[anywhere] * 5,
-        out_specs=anywhere,
+        in_specs=[hbm] * 5,
+        out_specs=pl.BlockSpec(memory_space=pltpu.VMEM),
         scratch_shapes=[
             pltpu.VMEM((tok, features), BF16),
             pltpu.VMEM((tok, features), BF16),
             pltpu.VMEM((tok, features), BF16),
             pltpu.VMEM((1, features), F32),
             pltpu.VMEM((chunks, planes, 2, rows, chunk), BF16),
-            pltpu.VMEM((chunks, 2 * tok, chunk), BF16),
             pltpu.VMEM((planes, 2, HEAD_DIM, width), BF16),
             pltpu.VMEM((planes, 2, HEAD_DIM, width), BF16),
             pltpu.VMEM((planes, 2, tok, width), BF16),
@@ -404,10 +407,9 @@
             dma((chunks,)),
             dma((chunks,)),
             dma((4,)),
-            dma((chunks,)),
         ],
         compiler_params=pltpu.CompilerParams(
-            collective_id=0, has_side_effects=True, vmem_limit_bytes=56 * 1024 * 1024
+            collective_id=0, has_side_effects=True, vmem_limit_bytes=40 * 1024 * 1024
         ),
     )(queries, keys, values, norm_gain.reshape(1, features), out_weight)
 

time: 59.9 us -> 64.1 us (1.070)
  local copies, waits for them, and re-layouts: 1.95 us -> 5.85 us
    unnamed x1 -> x11, local copies, waits for them, and re-layouts: 1.95 us -> 5.85 us
where the time goes in v5:
time: 64.1 us; the launch traced here: 63.7 us
  Pallas kernels  57.9 us (90%)
  local copies, waits for them, and re-layouts  5.85 us (9%)
    pallas_call x1, Pallas kernels, fused(): pl.pallas_call(functools.partial(kernel, planes, chunks), out_shape=jax.S...  57.9 us
    unnamed x11, local copies, waits for them, and re-layouts  5.85 us

profile of v5, /device:TPU:0, one launch (start us, length us, event | category | flops | bytes accessed | tf_op | source)
XLA Modules:
  0.0 63.7 jit_solution(16881847147609319414)
XLA Ops:
  0.0 0.0 copy-start
  0.0 1.1 %copy-done = bf16[104,3072]{1,0:T(8,128)(2,1)S(1)} copy-done((bf16[104,3072]{1,0:T(8,128)(2,1)S(1)}, bf16[104,3072]{1,0:T(8,128)(2,1)}, u32[]{:S(2)}) %copy-start) | copy-done | bytes 639000
  1.1 0.0 copy-start.1
  1.1 1.1 %copy-done.1 = bf16[104,3072]{1,0:T(8,128)(2,1)S(1)} copy-done((bf16[104,3072]{1,0:T(8,128)(2,1)S(1)}, bf16[104,3072]{1,0:T(8,128)(2,1)}, u32[]{:S(2)}) %copy-start.1) | copy-done | bytes 639000
  2.2 0.0 copy-start.2
  2.2 1.1 %copy-done.2 = bf16[104,3072]{1,0:T(8,128)(2,1)S(1)} copy-done((bf16[104,3072]{1,0:T(8,128)(2,1)S(1)}, bf16[104,3072]{1,0:T(8,128)(2,1)}, u32[]{:S(2)}) %copy-start.2) | copy-done | bytes 639000
  3.2 0.0 copy-start.3
  3.2 1.1 %copy-done.3 = bf16[192,1536]{1,0:T(8,128)(2,1)S(1)} copy-done((bf16[192,1536]{1,0:T(8,128)(2,1)S(1)}, bf16[192,1536]{1,0:T(8,128)(2,1)}, u32[]{:S(2)}) %copy-start.3) | copy-done | bytes 589848
  4.3 0.0 copy-start.4
  4.3 0.7 %copy-done.4 = f32[3072]{0:T(1024)S(1)} copy-done((f32[3072]{0:T(1024)S(1)}, f32[3072]{0:T(1024)}, u32[]{:S(2)}) %copy-start.4) | copy-done | bytes 12312
  5.0 57.9 %shard_map.55 = bf16[208,1536]{1,0:T(8,128)(2,1)S(1)} custom-call(bf16[104,3072]{1,0:T(8,128)(2,1)S(1)} %copy-done, bf16[104,3072]{1,0:T(8,128)(2,1)S(1)} %copy-done.1, bf16[104,3072]{1,0:T(8,128)(2,1)S(1)} %copy-done.2, f32[1,3072]{1,0:T(1,128)S(1)} %bitcast.1, bf16[192,1536]{1,0:T(8,128)(2,1)S(1)} %copy-done.3), custom_call_target="tpu_custom_call" | custom-call | tf_op jit(solution)/shard_map/pallas_call | solution.py:377
  62.9 0.8 %copy.7 = bf16[208,1536]{1,0:T(8,128)(2,1)} copy(bf16[208,1536]{1,0:T(8,128)(2,1)S(1)} %shard_map.55) | data formatting | bytes 1277952
Async XLA Ops:
  0.0 1.1 %copy-start = (bf16[104,3072]{1,0:T(8,128)(2,1)S(1)}, bf16[104,3072]{1,0:T(8,128)(2,1)}, u32[]{:S(2)}) copy-start(bf16[104,3072]{1,0:T(8,128)(2,1)} %q_in.1) | copy-start | bytes 1916932
  1.1 1.1 %copy-start.1 = (bf16[104,3072]{1,0:T(8,128)(2,1)S(1)}, bf16[104,3072]{1,0:T(8,128)(2,1)}, u32[]{:S(2)}) copy-start(bf16[104,3072]{1,0:T(8,128)(2,1)} %k_in.1) | copy-start | bytes 1916932
  2.2 1.1 %copy-start.2 = (bf16[104,3072]{1,0:T(8,128)(2,1)S(1)}, bf16[104,3072]{1,0:T(8,128)(2,1)}, u32[]{:S(2)}) copy-start(bf16[104,3072]{1,0:T(8,128)(2,1)} %v_in.1) | copy-start | bytes 1916932
  3.2 1.1 %copy-start.3 = (bf16[192,1536]{1,0:T(8,128)(2,1)S(1)}, bf16[192,1536]{1,0:T(8,128)(2,1)}, u32[]{:S(2)}) copy-start(bf16[192,1536]{1,0:T(8,128)(2,1)} %w_ref.1) | copy-start | bytes 1769476
  4.3 0.7 %copy-start.4 = (f32[3072]{0:T(1024)S(1)}, f32[3072]{0:T(1024)}, u32[]{:S(2)}) copy-start(f32[3072]{0:T(1024)} %param.8) | copy-start | bytes 36868

commit v6 on v2

--- a/solution.py
+++ b/solution.py
@@ -235,27 +235,20 @@
                 total = total + jnp.dot(scores, v * in_head16[h], preferred_element_type=F32)
             att[i, yy] = total
 
-            @pl.when(x == 0)
-            def _():
-                deliver(i, yy, att[i, yy])
-
-        pass_on_share(i, 1)
-
-    each(attend)
-
-    def attend_earlier(i):
-        @pl.when(x == 1)
-        def _():
-            for yy in range(2):
+            @pl.when(x == 1)
+            def _():
                 state_copy(i, yy).wait_recv()
                 state = state_in[i, yy]
                 wide = jnp.concatenate([state * m for m in in_head16], axis=0)
-                inter = jnp.dot(q_ref[:, columns(i, yy)], wide, preferred_element_type=F32)
-                deliver(i, yy, att[i, yy] + inter)
-
-        pass_on_share(i, 2)
-
-    each(attend_earlier)
+                att[i, yy] += jnp.dot(q, wide, preferred_element_type=F32)
+
+            deliver(i, yy, att[i, yy])
+
+        pass_on_share(i, 1)
+
+    each(attend)
+    every_chunk(lambda j: pass_on(j, 2))
+
     ms_copy = remote(ms.at[x], ms.at[x], ms_send, ms_recv, across)
     ms_copy.start()
 

time: 59.9 us -> 56.8 us (0.948)
  Pallas kernels: 57.7 us -> 54.6 us
    pallas_call x1, Pallas kernels: 57.7 us -> 54.6 us  [fused(): pl.pallas_call(functools.partial(kernel, planes, chunks), out_shape=jax.S...]
where the time goes in v6:
time: 56.8 us; the launch traced here: 56.6 us
  Pallas kernels  54.6 us (96%)
  local copies, waits for them, and re-layouts  1.95 us (3%)
    pallas_call x1, Pallas kernels, fused(): pl.pallas_call(functools.partial(kernel, planes, chunks), out_shape=jax.S...  54.6 us
    unnamed x1, local copies, waits for them, and re-layouts  1.95 us

profile of v6, /device:TPU:0, one launch (start us, length us, event | category | flops | bytes accessed | tf_op | source)
XLA Modules:
  0.0 56.6 jit_solution(6539905712403966891)
XLA Ops:
  0.0 54.6 %shard_map.55 = bf16[208,1536]{1,0:T(8,128)(2,1)} custom-call(bf16[104,3072]{1,0:T(8,128)(2,1)} %q_in.1, bf16[104,3072]{1,0:T(8,128)(2,1)} %k_in.1, bf16[104,3072]{1,0:T(8,128)(2,1)} %v_in.1, f32[1,3072]{1,0:T(1,128)} %bitcast.1, bf16[192,1536]{1,0:T(8,128)(2,1)} %w_ref.1), custom_call_target="tpu_custom_call" | custom-call | tf_op jit(solution)/shard_map/pallas_call | solution.py:366
  54.6 2.0 %copy.7 = bf16[208,1536]{1,0:T(8,128)(2,1)} copy(bf16[208,1536]{1,0:T(8,128)(2,1)} %shard_map.55) | data formatting | bytes 1277952

commit v7 on v6

--- a/solution.py
+++ b/solution.py
@@ -247,6 +247,8 @@
         pass_on_share(i, 1)
 
     each(attend)
+    for j in range(planes * (chunks // planes), chunks):
+        pass_on(j, 1)
     every_chunk(lambda j: pass_on(j, 2))
 
     ms_copy = remote(ms.at[x], ms.at[x], ms_send, ms_recv, across)
@@ -414,7 +416,7 @@
         P("fsdp", "ctx"),
     )
     planes = mesh.shape["fsdp"] // 4
-    chunks = planes
+    chunks = 6
 
     def body(queries, keys, values, norm_gain, out_weight):
         rows, out_columns = out_weight.shape

time: 56.8 us -> 58.3 us (1.026)
  Pallas kernels: 54.6 us -> 56.2 us
    pallas_call x1, Pallas kernels: 54.6 us -> 56.2 us  [fused(): pl.pallas_call(functools.partial(kernel, planes, chunks), out_shape=jax.S...]
where the time goes in v7:
time: 58.3 us; the launch traced here: 58.2 us
  Pallas kernels  56.2 us (96%)
  local copies, waits for them, and re-layouts  1.95 us (3%)
    pallas_call x1, Pallas kernels, fused(): pl.pallas_call(functools.partial(kernel, planes, chunks), out_shape=jax.S...  56.2 us
    unnamed x1, local copies, waits for them, and re-layouts  1.95 us

profile of v7, /device:TPU:0, one launch (start us, length us, event | category | flops | bytes accessed | tf_op | source)
XLA Modules:
  0.0 58.2 jit_solution(8715685575077797250)
XLA Ops:
  0.0 56.2 %shard_map.55 = bf16[208,1536]{1,0:T(8,128)(2,1)} custom-call(bf16[104,3072]{1,0:T(8,128)(2,1)} %q_in.1, bf16[104,3072]{1,0:T(8,128)(2,1)} %k_in.1, bf16[104,3072]{1,0:T(8,128)(2,1)} %v_in.1, f32[1,3072]{1,0:T(1,128)} %bitcast.1, bf16[192,1536]{1,0:T(8,128)(2,1)} %w_ref.1), custom_call_target="tpu_custom_call" | custom-call | tf_op jit(solution)/shard_map/pallas_call | solution.py:368
  56.2 2.0 %copy.7 = bf16[208,1536]{1,0:T(8,128)(2,1)} copy(bf16[208,1536]{1,0:T(8,128)(2,1)} %shard_map.55) | data formatting | bytes 1277952
